TPU v7x, 128 devices: a whole 4x4x4 slice. The times are simulated.
128 devices in a mesh: rows: 4 (over z_lo, core), cols: 32 (over y, x, z_hi).
Axes of the slice: x: 4, y: 4, z: 4 (z_hi: 2, z_lo: 2; z = z_hi * 2 + z_lo), core: 2. Of those that a mesh axis runs over, the one named last changes fastest.
Arguments:
- pair_integrals: float32 [4096, 16384], P('rows', 'cols'), may hold values from -6 to 6
- left_factor: float32 [4096, 1024], P('rows', 'cols'), may hold values from -0.9375 to 0.9375
- core: float32 [1024, 1024], replicated, may hold values from -6 to 6
- right_factor: float32 [16384, 1024], P('cols', 'rows'), may hold values from -0.46875 to 0.46875
Outputs:
- core_next: float32 [1024, 1024], replicated
All inputs are finite; a program needn't handle non-finite values.
Results may differ from a plain program's by a relative error of at most 0.000062.
Values sent between devices are 32-bit elements; how exact they have to be, the bound alone decides.
A program may use at most 128 MiB of HBM per device.

v0:
```python
import functools
import jax
import jax.numpy as jnp
from jax import lax
from jax.sharding import Mesh
from jax.sharding import PartitionSpec as P

COLS = ("cols_0", "cols_1", "cols_2")
ROWS = ("rows_0", "rows_1")
ROWS_COLS = ("rows_0", "rows_1", "cols_0", "cols_1", "cols_2")


def joined_along(parts, dim):
    shape = list(parts.shape[1:])
    shape[dim] *= parts.shape[0]
    return jnp.moveaxis(parts, 0, dim).reshape(shape)


def copy_for_each(x, axis):
    devices = lax.axis_size(axis)
    return lax.all_to_all(jnp.broadcast_to(x[None], (devices, *x.shape)), axis, 0, 0, tiled=True)


def gathered_copies(x, axis, dim):
    return joined_along(copy_for_each(x, axis), dim)


def one_axis_at_a_time(x, axes):
    return functools.reduce(lax.psum, axes, x)


def product(left, right):
    return jnp.dot(left, right, precision=lax.Precision.HIGHEST, preferred_element_type=jnp.float32)


def shards(pair_integrals, left_factor, core, right_factor):
    left_rows = lax.all_gather(left_factor, COLS, axis=1, tiled=True)
    right_rows = gathered_copies(right_factor, ROWS, 1)
    mixed = product(core, right_rows.T)
    residual = pair_integrals - product(left_rows, mixed)
    along = product(residual, right_rows)
    local_term = product(left_rows.T, along)
    gradient = lax.psum(local_term, ROWS_COLS)
    numer = jnp.sum(gradient * gradient)
    image = product(left_rows, product(gradient, right_rows.T))
    denom = one_axis_at_a_time(jnp.sum(image * image), ROWS_COLS)
    return core + numer / denom * gradient


def solution(mesh):
    finer = Mesh(
        mesh.devices.reshape(2, 2, 4, 4, 2), ("rows_0", "rows_1", "cols_0", "cols_1", "cols_2")
    )
    placed = (P(ROWS, COLS), P(ROWS, COLS), P(), P(COLS, ROWS))
    return jax.shard_map(shards, mesh=finer, in_specs=placed, out_specs=P(), check_vma=False)
```

profile of v0, /device:TPU:0, one launch (start us, length us, event | category | flops | bytes accessed | tf_op | source)
XLA Modules:
  0.0 376.6 jit_solution(10287196216406322099)
XLA Ops:
  6.5 0.0 all-gather.2.cloned.1.call-start
  6.5 0.7 all-gather.2.cloned.1.call-update
  7.3 0.0 all-reduce.2.cloned.1.call-start
  7.3 1.2 copy.7
  8.5 0.0 copy-start
  8.6 0.3 broadcast_in_dim.2
  8.8 30.0 %all_to_all.5 = f32[4,512,256]{1,2,0:T(8,128)S(1)} all-to-all(f32[4,512,256]{1,2,0:T(8,128)S(1)} %broadcast_in_dim.2), channel_id=1, replica_groups=mesh['rows_0'=2,'rows_1'=2,'cols_0'=4,'cols_1'=4,'cols_2'=2] {'rows_0','..., dimensions={0} | all-to-all | bytes 4194304 | tf_op jit(solution)/shard_map/all_to_all | solution.py:21
  38.8 0.0 copy-done
  38.8 8.0 %fusion.1 = f32[1024,512]{1,0:T(8,128)} fusion(f32[1024,1024]{1,0:T(8,128)S(1)} %copy-done, f32[512,1024]{0,1:T(8,128)S(1)} %bitcast.19), kind=kOutput, calls=%fused_computation.6 | convolution fusion | flops 6442450944 | bytes 8388608 | tf_op jit(solution)/shard_map/dot_general | solution.py:33
  46.8 48.8 %all-gather.2.cloned.1.call-done = f32[1024,1024]{0,1:T(8,128)} async-done(((f32[1024,32]{0,1:T(8,128)}), f32[1024,1024]{0,1:T(8,128)}) %all-gather.2.cloned.1.call-update) | async-done | bytes 4194320 | tf_op jit(solution)/shard_map/all_gather | solution.py:37
  95.6 0.0 copy-start.3
  95.6 9.9 %fusion.2 = f32[512,1024]{0,1:T(8,128)S(1)} fusion(f32[1024,512]{1,0:T(8,128)} %fusion.1, f32[1024,1024]{0,1:T(8,128)} %all-gather.2.cloned.1.call-done), kind=kOutput, calls=%fused_computation.7 | convolution fusion | flops 6442450944 | bytes 8388608 | tf_op jit(solution)/shard_map/dot_general | solution.py:33
  105.6 0.0 copy-done.3
  105.6 0.0 copy-start.1
  105.6 6.9 %fusion = f32[1024,1024]{1,0:T(8,128)S(1)} fusion(f32[512,1024]{0,1:T(8,128)S(1)} %bitcast.20, f32[1024,512]{1,0:T(8,128)S(1)} %copy-done.3, f32[512,1024]{0,1:T(8,128)S(1)} %fusion.2), kind=kOutput, calls=%fused_computation.4 | convolution fusion | flops 6442975232 | bytes 10485760 | tf_op jit(solution)/shard_map/dot_general | solution.py:33
  112.5 0.0 copy-done.1
  112.5 29.8 %convolution_bitcast_fusion = f32[1024,1024]{0,1:T(8,128)} fusion(f32[1024,1024]{1,0:T(8,128)S(1)} %fusion, f32[1024,1024]{0,1:T(8,128)S(1)} %copy-done.1), kind=kOutput, calls=%fused_computation.2 | convolution fusion | flops 12884901888 | bytes 12582912 | tf_op jit(solution)/shard_map/dot_general | solution.py:33
  142.3 0.0 all-reduce.2.cloned.1.call-update
  142.3 150.9 %all-reduce.2.cloned.1.call-done = f32[1024,1024]{0,1:T(8,128)} async-done(((f32[1024,1024]{0,1:T(8,128)}), f32[1024,1024]{0,1:T(8,128)}) %all-reduce.2.cloned.1.call-update) | async-done | bytes 4194320 | tf_op jit(solution)/shard_map/psum | solution.py:43
  293.2 0.0 copy-start.2
  293.2 8.8 %fusion.3 = f32[1024,512]{1,0:T(8,128)S(1)} fusion(f32[1024,1024]{0,1:T(8,128)} %all-reduce.2.cloned.1.call-done, f32[512,1024]{0,1:T(8,128)S(1)} %bitcast.21), kind=kOutput, calls=%fused_computation.8 | convolution fusion | flops 6442450944 | bytes 8388608 | tf_op jit(solution)/shard_map/dot_general | solution.py:33
  302.0 0.0 copy-done.2
  302.0 7.8 %multiply_reduce_fusion.1 = f32[]{:T(128)} fusion(f32[1024,512]{1,0:T(8,128)S(1)} %fusion.3, f32[1024,1024]{0,1:T(8,128)S(1)} %copy-done.2), kind=kOutput, calls=%fused_computation.5 | convolution fusion | flops 6443499520 | bytes 6291460 | tf_op jit(solution)/shard_map/dot_general | solution.py:33
  309.8 5.5 %psum.43 = f32[]{:T(128)} all-reduce(f32[]{:T(128)} %multiply_reduce_fusion.1), channel_id=1, replica_groups=mesh['rows_0'=2,'rows_1'=2,'cols_0'=4,'cols_1'=4,'cols_2'=2] {'rows_0'}, use_global_device_ids=true, to_apply=%region_3.0 | all-reduce | flops 1 | bytes 8 | tf_op jit(solution)/shard_map/psum | solution.py:29
  315.4 3.1 psum.44
  318.4 10.2 %psum.45 = f32[]{:T(128)} all-reduce(f32[]{:T(128)} %psum.44), channel_id=1, replica_groups=mesh['rows_0'=2,'rows_1'=2,'cols_0'=4,'cols_1'=4,'cols_2'=2] {'cols_0'}, use_global_device_ids=true, to_apply=%region_5.0 | all-reduce | flops 1 | bytes 8 | tf_op jit(solution)/shard_map/psum | solution.py:29
  328.7 11.1 %psum.46 = f32[]{:T(128)} all-reduce(f32[]{:T(128)} %psum.45), channel_id=1, replica_groups=mesh['rows_0'=2,'rows_1'=2,'cols_0'=4,'cols_1'=4,'cols_2'=2] {'cols_1'}, use_global_device_ids=true, to_apply=%region_6.0 | all-reduce | flops 1 | bytes 8 | tf_op jit(solution)/shard_map/psum | solution.py:29
  339.8 5.3 %copy.8 = f32[1024,1024]{0,1:T(8,128)} copy(f32[1024,1024]{1,0:T(8,128)} %param.6) | data formatting | bytes 8388608 | tf_op args[2]
  345.1 7.1 %psum.47 = f32[]{:T(128)} all-reduce(f32[]{:T(128)} %psum.46), channel_id=1, replica_groups=mesh['rows_0'=2,'rows_1'=2,'cols_0'=4,'cols_1'=4,'cols_2'=2] {'cols_2'}, use_global_device_ids=true, to_apply=%region_7.0 | all-reduce | flops 1 | bytes 8 | tf_op jit(solution)/shard_map/psum | solution.py:29
  352.2 3.9 %multiply_reduce_fusion = f32[]{:T(128)} fusion(f32[1024,1024]{0,1:T(8,128)} %all-reduce.2.cloned.1.call-done), kind=kLoop, calls=%fused_computation.1 | loop fusion | flops 2097151 | bytes 4194308 | tf_op jit(solution)/shard_map/reduce_sum | solution.py:44
  357.3 6.9 %multiply_add_fusion = f32[1024,1024]{0,1:T(8,128)} fusion(f32[1024,1024]{0,1:T(8,128)} %copy.8, f32[1024,1024]{0,1:T(8,128)} %all-reduce.2.cloned.1.call-done, f32[]{:T(128)S(6)} %div.3), kind=kLoop, calls=%fused_computation | loop fusion | flops 2097152 | bytes 12582916 | tf_op jit(solution)/shard_map/add | solution.py:47
  364.2 5.3 %copy.9 = f32[1024,1024]{1,0:T(8,128)} copy(f32[1024,1024]{0,1:T(8,128)} %multiply_add_fusion) | data formatting | bytes 8388608 | tf_op jit(solution)/shard_map/add | solution.py:47
Async XLA Ops:
  6.5 89.1 %all-gather.2.cloned.1.call-start = ((), (), s32[]{:S(2)}) async-start(), calls=%async_computation.1 | async-start | bytes 4325376 | tf_op jit(solution)/shard_map/all_gather | solution.py:37
  7.3 286.0 %all-reduce.2.cloned.1.call-start = ((), (), s32[]{:S(2)}) async-start(), calls=%async_computation.2 | async-start | bytes 8388608 | tf_op jit(solution)/shard_map/psum | solution.py:43
  8.5 30.2 %copy-start = (f32[1024,1024]{1,0:T(8,128)S(1)}, f32[1024,1024]{1,0:T(8,128)}, u32[]{:S(2)}) copy-start(f32[1024,1024]{1,0:T(8,128)} %param.6) | copy-start | bytes 12582916
  95.6 9.9 %copy-start.3 = (f32[1024,512]{1,0:T(8,128)S(1)}, f32[1024,512]{1,0:T(8,128)}, u32[]{:S(2)}) copy-start(f32[1024,512]{1,0:T(8,128)} %param.4) | copy-start | bytes 6291460
  105.6 6.9 %copy-start.1 = (f32[1024,1024]{0,1:T(8,128)S(1)}, f32[1024,1024]{0,1:T(8,128)}, u32[]{:S(2)}) copy-start(f32[1024,1024]{0,1:T(8,128)} %all-gather.2.cloned.1.call-done) | copy-start | bytes 12582916
  293.2 8.8 %copy-start.2 = (f32[1024,1024]{0,1:T(8,128)S(1)}, f32[1024,1024]{0,1:T(8,128)}, u32[]{:S(2)}) copy-start(f32[1024,1024]{0,1:T(8,128)} %all-gather.2.cloned.1.call-done) | copy-start | bytes 12582916
Sparse Core Ops, SparseCore 0:
  10.3 85.2 all-gather.1
  142.4 150.7 all-reduce.1
where the time goes:
time: 384 us; the launch traced here: 377 us
  waiting for transfers between devices  201 us (52%)
  matrix products  71.1 us (19%)
  blocking collectives  67 us (17%)
  between operations  15 us (4%)
  local copies, waits for them, and re-layouts  12.2 us (3%)
  other arithmetic  10.7 us (3%)
    psum x1, waiting for transfers between devices, shards(): gradient = lax.psum(local_term, ROWS_COLS)  151 us
    dot_general x6, matrix products, product(): jnp.dot(left, right, precision=lax.Precision.HIGHEST, preferred_element_t...  71.1 us
    all_gather x1, waiting for transfers between devices, shards(): left_rows = lax.all_gather(left_factor, COLS, axis=1, tiled=True)  48.8 us
    psum x5, blocking collectives, one_axis_at_a_time(): return functools.reduce(lax.psum, axes, x)  37.1 us
    all_to_all x1, blocking collectives, copy_for_each(): lax.all_to_all(jnp.broadcast_to(x[None], (devices, *x.shape)), axis, 0, 0...  30 us
  transfers between devices with their start and end apart: 2, of which 2 were waited for; matrix products, arithmetic and copies ran while one was open for 3% of the time, Pallas kernels for 0%

commit v1 on v0

--- a/solution.py
+++ b/solution.py
@@ -34,7 +34,9 @@
 
 
 def shards(pair_integrals, left_factor, core, right_factor):
-    left_rows = lax.all_gather(left_factor, COLS, axis=1, tiled=True)
+    left_rows = jnp.concatenate(
+        lax.all_to_all(jnp.stack([left_factor] * lax.axis_size(COLS), axis=0), COLS, 0, 0), 1
+    )
     right_rows = gathered_copies(right_factor, ROWS, 1)
     mixed = product(core, right_rows.T)
     residual = pair_integrals - product(left_rows, mixed)

time: 384 us -> 403 us (1.049)
  starting transfers between devices: 0.04 us -> 10.5 us
  matrix products: 71.1 us -> 76.3 us
    all_to_all x0 -> x1, waiting for transfers between devices: none -> 50.7 us  [shards(): lax.all_to_all(jnp.stack([left_factor] * lax.axis_size(COLS), axis=0), CO...]
    all_gather x1 -> x0, waiting for transfers between devices: 48.8 us -> none  [shards(): left_rows = lax.all_gather(left_factor, COLS, axis=1, tiled=True)]
    all_to_all x0 -> x1, starting transfers between devices: none -> 10.5 us  [shards(): lax.all_to_all(jnp.stack([left_factor] * lax.axis_size(COLS), axis=0), CO...]
    dot_general x6, matrix products: 71.1 us -> 76.3 us  [product(): jnp.dot(left, right, precision=lax.Precision.HIGHEST, preferred_element_t...]
  transfers between devices with their start and end apart: 2 -> 2, of which waited for: 2 -> 2; matrix products, arithmetic and copies ran while one was open for 3% -> 2% of each run, Pallas kernels for 0% -> 0%
where the time goes in v1:
time: 403 us; the launch traced here: 396 us
  waiting for transfers between devices  203 us (50%)
  matrix products  76.3 us (19%)
  blocking collectives  65.8 us (16%)
  between operations  15 us (4%)
  local copies, waits for them, and re-layouts  14.8 us (4%)
  other arithmetic  10.7 us (3%)
  starting transfers between devices  10.5 us (3%)
    psum x1, waiting for transfers between devices, shards(): gradient = lax.psum(local_term, ROWS_COLS)  152 us
    dot_general x6, matrix products, product(): jnp.dot(left, right, precision=lax.Precision.HIGHEST, preferred_element_t...  76.3 us
    all_to_all x1, waiting for transfers between devices, shards(): lax.all_to_all(jnp.stack([left_factor] * lax.axis_size(COLS), axis=0), CO...  50.7 us
    psum x5, blocking collectives, one_axis_at_a_time(): return functools.reduce(lax.psum, axes, x)  37.1 us
    all_to_all x1, blocking collectives, copy_for_each(): lax.all_to_all(jnp.broadcast_to(x[None], (devices, *x.shape)), axis, 0, 0...  28.8 us
    all_to_all x1, starting transfers between devices, shards(): lax.all_to_all(jnp.stack([left_factor] * lax.axis_size(COLS), axis=0), CO...  10.5 us
  transfers between devices with their start and end apart: 2, of which 2 were waited for; matrix products, arithmetic and copies ran while one was open for 2% of the time, Pallas kernels for 0%

profile of v1, /device:TPU:0, one launch (start us, length us, event | category | flops | bytes accessed | tf_op | source)
XLA Modules:
  0.0 396.3 jit_solution(2036621160203371787)
XLA Ops:
  6.5 0.0 copy-start.1
  6.5 1.3 copy.8
  7.8 0.3 broadcast_in_dim.2
  8.1 28.8 %all_to_all.10 = f32[4,512,256]{1,2,0:T(8,128)S(1)} all-to-all(f32[4,512,256]{1,2,0:T(8,128)S(1)} %broadcast_in_dim.2), channel_id=1, replica_groups=mesh['rows_0'=2,'rows_1'=2,'cols_0'=4,'cols_1'=4,'cols_2'=2] {'rows_0','..., dimensions={0} | all-to-all | bytes 4194304 | tf_op jit(solution)/shard_map/all_to_all | solution.py:21
  36.9 0.0 copy-done.1
  36.9 2.5 stack.2
  39.4 10.5 %all-to-all-start.1 = ((f32[32,1024,32]{1,2,0:T(8,128)}), f32[32,1024,32]{1,2,0:T(8,128)}, u32[]{:S(2)}, u32[]{:S(2)}) async-start(f32[32,1024,32]{1,2,0:T(8,128)} %stack.2), calls=%async_computation.1 | async-start | bytes 8388608 | tf_op jit(solution)/shard_map/all_to_all | solution.py:38
  49.9 0.0 all-reduce.2.cloned.1.call-start
  49.9 9.7 %fusion.1 = f32[1024,512]{1,0:T(8,128)} fusion(f32[1024,1024]{1,0:T(8,128)} %param.6, f32[512,1024]{0,1:T(8,128)S(1)} %bitcast.22), kind=kOutput, calls=%fused_computation.6 | convolution fusion | flops 6442450944 | bytes 8388608 | tf_op jit(solution)/shard_map/dot_general | solution.py:33
  59.6 50.7 %all-to-all-done.1 = f32[32,1024,32]{1,2,0:T(8,128)} async-done(((f32[32,1024,32]{1,2,0:T(8,128)}), f32[32,1024,32]{1,2,0:T(8,128)}, u32[]{:S(2)}, u32[]{:S(2)}) %all-to-all-start.1) | async-done | bytes 4194336 | tf_op jit(solution)/shard_map/all_to_all | solution.py:38
  110.3 0.0 copy-start
  110.3 9.9 %fusion.2 = f32[512,1024]{0,1:T(8,128)S(1)} fusion(f32[1024,512]{1,0:T(8,128)} %fusion.1, f32[1024,1024]{0,1:T(8,128)} %bitcast.3), kind=kOutput, calls=%fused_computation.7 | convolution fusion | flops 6442450944 | bytes 8388608 | tf_op jit(solution)/shard_map/dot_general | solution.py:33
  120.2 0.0 copy-done
  120.2 6.9 %fusion = f32[1024,1024]{1,0:T(8,128)S(1)} fusion(f32[512,1024]{0,1:T(8,128)S(1)} %bitcast.23, f32[1024,512]{1,0:T(8,128)S(1)} %copy-done, f32[512,1024]{0,1:T(8,128)S(1)} %fusion.2), kind=kOutput, calls=%fused_computation.4 | convolution fusion | flops 6442975232 | bytes 10485760 | tf_op jit(solution)/shard_map/dot_general | solution.py:33
  127.1 31.5 %convolution_bitcast_fusion = f32[1024,1024]{0,1:T(8,128)} fusion(f32[1024,1024]{1,0:T(8,128)S(1)} %fusion, f32[1024,1024]{0,1:T(8,128)} %bitcast.3), kind=kOutput, calls=%fused_computation.2 | convolution fusion | flops 12884901888 | bytes 12582912 | tf_op jit(solution)/shard_map/dot_general | solution.py:33
  158.6 0.0 all-reduce.2.cloned.1.call-update
  158.7 152.4 %all-reduce.2.cloned.1.call-done = f32[1024,1024]{0,1:T(8,128)} async-done(((f32[1024,1024]{0,1:T(8,128)}), f32[1024,1024]{0,1:T(8,128)}) %all-reduce.2.cloned.1.call-update) | async-done | bytes 4194320 | tf_op jit(solution)/shard_map/psum | solution.py:45
  311.1 8.6 %fusion.3 = f32[1024,512]{1,0:T(8,128)S(1)} fusion(f32[1024,1024]{0,1:T(8,128)} %all-reduce.2.cloned.1.call-done, f32[512,1024]{0,1:T(8,128)S(1)} %bitcast.24), kind=kOutput, calls=%fused_computation.8 | convolution fusion | flops 6442450944 | bytes 8388608 | tf_op jit(solution)/shard_map/dot_general | solution.py:33
  319.7 9.7 %multiply_reduce_fusion.1 = f32[]{:T(128)} fusion(f32[1024,512]{1,0:T(8,128)S(1)} %fusion.3, f32[1024,1024]{0,1:T(8,128)} %bitcast.3), kind=kOutput, calls=%fused_computation.5 | convolution fusion | flops 6443499520 | bytes 6291460 | tf_op jit(solution)/shard_map/dot_general | solution.py:33
  329.4 5.5 %psum.43 = f32[]{:T(128)} all-reduce(f32[]{:T(128)} %multiply_reduce_fusion.1), channel_id=1, replica_groups=mesh['rows_0'=2,'rows_1'=2,'cols_0'=4,'cols_1'=4,'cols_2'=2] {'rows_0'}, use_global_device_ids=true, to_apply=%region_3.0 | all-reduce | flops 1 | bytes 8 | tf_op jit(solution)/shard_map/psum | solution.py:29
  335.0 3.1 psum.44
  338.1 10.2 %psum.45 = f32[]{:T(128)} all-reduce(f32[]{:T(128)} %psum.44), channel_id=1, replica_groups=mesh['rows_0'=2,'rows_1'=2,'cols_0'=4,'cols_1'=4,'cols_2'=2] {'cols_0'}, use_global_device_ids=true, to_apply=%region_5.0 | all-reduce | flops 1 | bytes 8 | tf_op jit(solution)/shard_map/psum | solution.py:29
  348.3 11.1 %psum.46 = f32[]{:T(128)} all-reduce(f32[]{:T(128)} %psum.45), channel_id=1, replica_groups=mesh['rows_0'=2,'rows_1'=2,'cols_0'=4,'cols_1'=4,'cols_2'=2] {'cols_1'}, use_global_device_ids=true, to_apply=%region_6.0 | all-reduce | flops 1 | bytes 8 | tf_op jit(solution)/shard_map/psum | solution.py:29
  359.4 5.3 %copy.9 = f32[1024,1024]{0,1:T(8,128)} copy(f32[1024,1024]{1,0:T(8,128)} %param.6) | data formatting | bytes 8388608 | tf_op args[2]
  364.8 7.1 %psum.47 = f32[]{:T(128)} all-reduce(f32[]{:T(128)} %psum.46), channel_id=1, replica_groups=mesh['rows_0'=2,'rows_1'=2,'cols_0'=4,'cols_1'=4,'cols_2'=2] {'cols_2'}, use_global_device_ids=true, to_apply=%region_7.0 | all-reduce | flops 1 | bytes 8 | tf_op jit(solution)/shard_map/psum | solution.py:29
  371.8 3.9 multiply_reduce_fusion
  377.0 6.9 %multiply_add_fusion = f32[1024,1024]{0,1:T(8,128)} fusion(f32[1024,1024]{0,1:T(8,128)} %copy.9, f32[1024,1024]{0,1:T(8,128)} %all-reduce.2.cloned.1.call-done, f32[]{:T(128)S(6)} %div.3), kind=kLoop, calls=%fused_computation | loop fusion | flops 2097152 | bytes 12582916 | tf_op jit(solution)/shard_map/add | solution.py:49
  383.9 5.3 %copy.10 = f32[1024,1024]{1,0:T(8,128)} copy(f32[1024,1024]{0,1:T(8,128)} %multiply_add_fusion) | data formatting | bytes 8388608 | tf_op jit(solution)/shard_map/add | solution.py:49
Async XLA Ops:
  6.5 30.3 %copy-start.1 = (f32[1024,32]{0,1:T(8,128)S(1)}, f32[1024,32]{0,1:T(8,128)}, u32[]{:S(2)}) copy-start(f32[1024,32]{0,1:T(8,128)} %param.5) | copy-start | bytes 393220
  39.4 70.9 %all-to-all-start.1 = ((f32[32,1024,32]{1,2,0:T(8,128)}), f32[32,1024,32]{1,2,0:T(8,128)}, u32[]{:S(2)}, u32[]{:S(2)}) async-start(f32[32,1024,32]{1,2,0:T(8,128)} %stack.2), calls=%async_computation.1 | async-start | bytes 8388608 | tf_op jit(solution)/shard_map/all_to_all | solution.py:38
  49.9 261.2 %all-reduce.2.cloned.1.call-start = ((), (), s32[]{:S(2)}) async-start(), calls=%async_computation.2 | async-start | bytes 8388608 | tf_op jit(solution)/shard_map/psum | solution.py:45
  110.3 9.9 %copy-start = (f32[1024,512]{1,0:T(8,128)S(1)}, f32[1024,512]{1,0:T(8,128)}, u32[]{:S(2)}) copy-start(f32[1024,512]{1,0:T(8,128)} %param.4) | copy-start | bytes 6291460
Sparse Core Ops, SparseCore 0:
  158.8 152.2 all-reduce.1
